TPU v7x, 32 devices: a whole 2x2x4 slice. The times are simulated.
32 devices in a mesh: fsdp: 4 (over x, core), tp: 8 (over z, y).
Axes of the slice: x: 2, y: 2, z: 4, core: 2. Of those that a mesh axis runs over, the one named last changes fastest.
Arguments:
- tokens: bfloat16 [1024, 2560], P(('fsdp', 'tp')), may hold values from -6 to 6
- cotangent: bfloat16 [1024, 14336], P('fsdp', 'tp'), may hold values from -48 to 48
- up_branch: bfloat16 [1024, 14336], P('fsdp', 'tp'), may hold values from -6 to 6
- gate_weight: bfloat16 [2560, 14336], P('fsdp', 'tp'), may hold values from -0.125 to 0.125
- probe: bfloat16 [2560, 14336], P('fsdp', 'tp'), may hold values from -5 to 5
- hess_ema: float32 [2560, 14336], P('fsdp', 'tp'), may hold values from -6 to 6
Outputs:
- hess_diag: float32 [2560, 14336], P('fsdp', 'tp')
- ema_next: float32 [2560, 14336], P('fsdp', 'tp')
All inputs are finite; a program needn't handle non-finite values.
Results may differ from a plain program's by a relative error of at most 0.015.
Values may be sent and summed in bfloat16 or wider, within the bound.
A program may use at most 128 MiB of HBM per device.

v0:
```python
import jax
import jax.numpy as jnp
from jax import lax
from jax.sharding import PartitionSpec as P


def body(tokens, cotangent, up_branch, gate_weight, probe, hess_ema):
    groups = lax.axis_size("fsdp")
    rows = gate_weight.shape[0]
    pieces = tokens.reshape(tokens.shape[0], groups, rows).transpose(1, 0, 2)
    pieces = lax.all_to_all(pieces, "fsdp", 0, 0, tiled=True)
    whole = lax.all_gather(pieces, "tp", axis=1, tiled=True).reshape(-1, rows)
    total_tokens = whole.shape[0]

    def summed(weight):
        part = jnp.dot(whole, weight, preferred_element_type=jnp.float32)
        return lax.psum_scatter(
            part.astype(jnp.bfloat16), "fsdp", scatter_dimension=0, tiled=True
        ).astype(jnp.float32)

    gate = summed(gate_weight)
    tangent = summed(probe)
    sig = jax.nn.sigmoid(gate)
    second = sig * (1.0 - sig) * (2.0 + gate * (1.0 - 2.0 * sig))
    weighted = (
        cotangent.astype(jnp.float32)
        * up_branch.astype(jnp.float32)
        * second
        * tangent
        / total_tokens
    ).astype(jnp.bfloat16)
    every = lax.all_gather(weighted, "fsdp", axis=0, tiled=True)
    hvp = lax.dot_general(
        whole, every, (((0,), (0,)), ((), ())), preferred_element_type=jnp.float32
    )
    hess_diag = probe.astype(jnp.float32) * hvp
    ema_next = 0.99 * hess_ema + 0.01 * hess_diag
    return (hess_diag, ema_next)


def solution(mesh):
    placed = (
        P(("fsdp", "tp"), None),
        P("fsdp", "tp"),
        P("fsdp", "tp"),
        P("fsdp", "tp"),
        P("fsdp", "tp"),
        P("fsdp", "tp"),
    )
    return jax.shard_map(
        body,
        mesh=mesh,
        in_specs=placed,
        out_specs=(P("fsdp", "tp"), P("fsdp", "tp")),
        check_vma=False,
    )
```

profile of v0, /device:TPU:0, one launch (start us, length us, event | category | flops | bytes accessed | tf_op | source)
XLA Modules:
  0.0 216.9 jit_solution(8730116425908383532)
XLA Ops:
  7.2 0.0 copy-start
  7.2 0.0 all-gather.3.cloned.1.call-start
  7.2 1.1 reshape.10
  8.4 9.0 %all_to_all.5 = bf16[4,32,640]{2,1,0:T(8,128)(2,1)S(1)} all-to-all(bf16[4,32,640]{2,1,0:T(8,128)(2,1)S(1)} %copy.22), channel_id=1, replica_groups=mesh['fsdp'=4,'tp'=8] {'fsdp'}, dimensions={0} | all-to-all | bytes 327680 | tf_op jit(solution)/shard_map/all_to_all | solution.py:11
  17.4 0.8 copy.23
  18.1 0.0 all-gather.3.cloned.1.call-update
  18.1 0.0 reduce-scatter.5.cloned.1.call-start
  18.2 42.2 %all-gather.3.cloned.1.call-done = bf16[4,256,640]{2,0,1:T(4,128)(2,1)} async-done(((bf16[4,32,640]{2,0,1:T(4,128)(2,1)}), bf16[4,256,640]{2,0,1:T(4,128)(2,1)}) %all-gather.3.cloned.1.call-update) | async-done | bytes 1310736 | tf_op jit(solution)/shard_map/all_gather | solution.py:12
  60.4 0.0 copy-start.2
  60.4 1.6 copy.24
  62.0 0.0 copy-start.1
  62.0 1.0 copy-done.1
  63.1 0.0 copy-done.2
  63.1 4.4 %convolution_convert_fusion = bf16[1024,1792]{1,0:T(8,128)(2,1)} fusion(bf16[1024,640]{1,0:T(8,128)(2,1)S(1)} %bitcast.10, bf16[640,1792]{1,0:T(8,128)(2,1)S(1)} %copy-done.2), kind=kOutput, calls=%fused_computation.2 | convolution fusion | flops 2350645248 | bytes 7274496 | tf_op jit(solution)/shard_map/dot_general | solution.py:16
  67.5 0.0 reduce-scatter.5.cloned.1.call-update
  67.5 0.0 reduce-scatter.3.cloned.1.call-start
  67.6 0.0 copy-done
  67.6 6.0 %convolution_convert_fusion.1 = bf16[1024,1792]{1,0:T(8,128)(2,1)} fusion(bf16[1024,640]{1,0:T(8,128)(2,1)} %bitcast.11, bf16[640,1792]{1,0:T(8,128)(2,1)S(1)} %copy-done), kind=kOutput, calls=%fused_computation.3 | convolution fusion | flops 2350645248 | bytes 7274496 | tf_op jit(solution)/shard_map/dot_general | solution.py:16
  73.6 0.0 copy-start.3
  73.6 0.0 reduce-scatter.3.cloned.1.call-update
  73.6 0.0 all-gather.5.cloned.1.call-start
  73.7 33.9 %reduce-scatter.5.cloned.1.call-done = bf16[256,1792]{1,0:T(8,128)(2,1)} async-done(((bf16[1024,1792]{1,0:T(8,128)(2,1)}), bf16[256,1792]{1,0:T(8,128)(2,1)}) %reduce-scatter.5.cloned.1.call-update) | async-done | bytes 917520 | tf_op jit(solution)/shard_map/reduce_scatter | solution.py:17
  107.6 44.6 %reduce-scatter.3.cloned.1.call-done = bf16[256,1792]{1,0:T(8,128)(2,1)} async-done(((bf16[1024,1792]{1,0:T(8,128)(2,1)}), bf16[256,1792]{1,0:T(8,128)(2,1)}) %reduce-scatter.3.cloned.1.call-update) | async-done | bytes 917520 | tf_op jit(solution)/shard_map/reduce_scatter | solution.py:17
  152.2 0.0 copy-done.3
  152.2 3.8 %fusion.8 = bf16[256,1792]{1,0:T(8,128)(2,1)} fusion(bf16[256,1792]{1,0:T(8,128)(2,1)} %reduce-scatter.3.cloned.1.call-done, bf16[256,1792]{1,0:T(8,128)(2,1)} %reduce-scatter.5.cloned.1.call-done, bf16[256,1792]{1,0:T(8,128)(2,1)S(1)} %copy-done.3, bf16[256,1792]{1,0:T(8,128)(2,1)} %param.7), kind=kLoop, calls=%fused_computation.15 | loop fusion | flops 8716288 | bytes 4587520 | tf_op jit(solution)/shard_map/convert_element_type | solution.py:31
  156.0 0.0 all-gather.5.cloned.1.call-update
  156.0 4.2 %copy.21 = bf16[640,1792]{0,1:T(8,128)(2,1)} copy(bf16[640,1792]{1,0:T(8,128)(2,1)} %param.10) | data formatting | bytes 4587520 | tf_op args[4]
  160.2 5.7 %copy.25 = f32[640,1792]{0,1:T(8,128)} copy(f32[640,1792]{1,0:T(8,128)} %param.11) | data formatting | bytes 9175040 | tf_op args[5]
  166.0 21.7 %all-gather.5.cloned.1.call-done = bf16[1024,1792]{1,0:T(8,128)(2,1)} async-done(((bf16[256,1792]{1,0:T(8,128)(2,1)}), bf16[1024,1792]{1,0:T(8,128)(2,1)}) %all-gather.5.cloned.1.call-update) | async-done | bytes 3670032 | tf_op jit(solution)/shard_map/all_gather | solution.py:32
  187.7 11.4 %multiply_add_fusion = (f32[640,1792]{0,1:T(8,128)}, f32[640,1792]{0,1:T(8,128)}) fusion(f32[640,1792]{0,1:T(8,128)} %copy.25, bf16[1024,1792]{1,0:T(8,128)(2,1)} %all-gather.5.cloned.1.call-done, bf16[1024,640]{1,0:T(8,128)(2,1)} %bitcast.12, bf16[640,1792]{0,1:T(8,128)(2,1)} %copy.21), kind=kOutput, calls=%fused_computation.1 | convolution fusion | flops 2354544640 | bytes 21037056 | tf_op jit(solution)/shard_map/dot_general | solution.py:33
  199.1 5.7 %copy.27 = f32[640,1792]{1,0:T(8,128)} copy(f32[640,1792]{0,1:T(8,128)} %get-tuple-element.10) | data formatting | bytes 9175040
  204.7 5.7 %copy.26 = f32[640,1792]{1,0:T(8,128)} copy(f32[640,1792]{0,1:T(8,128)} %get-tuple-element.11) | data formatting | bytes 9175040
  (1 shorter events, 0.0 us)
Async XLA Ops:
  7.2 60.4 %copy-start = (bf16[640,1792]{1,0:T(8,128)(2,1)S(1)}, bf16[640,1792]{1,0:T(8,128)(2,1)}, u32[]{:S(2)}) copy-start(bf16[640,1792]{1,0:T(8,128)(2,1)} %param.9) | copy-start | bytes 6881284
  7.2 53.2 %all-gather.3.cloned.1.call-start = ((), (), s32[]{:S(2)}) async-start(), calls=%async_computation.3 | async-start | bytes 1474560 | tf_op jit(solution)/shard_map/all_gather | solution.py:12
  18.1 89.4 %reduce-scatter.5.cloned.1.call-start = ((), (), s32[]{:S(2)}) async-start(), calls=%async_computation.5 | async-start | bytes 4587520 | tf_op jit(solution)/shard_map/reduce_scatter | solution.py:17
  60.4 2.7 %copy-start.2 = (bf16[640,1792]{1,0:T(8,128)(2,1)S(1)}, bf16[640,1792]{1,0:T(8,128)(2,1)}, u32[]{:S(2)}) copy-start(bf16[640,1792]{1,0:T(8,128)(2,1)} %param.10) | copy-start | bytes 6881284
  62.0 1.1 copy-start.1
  67.5 84.6 %reduce-scatter.3.cloned.1.call-start = ((), (), s32[]{:S(2)}) async-start(), calls=%async_computation.4 | async-start | bytes 4587520 | tf_op jit(solution)/shard_map/reduce_scatter | solution.py:17
  73.6 78.5 %copy-start.3 = (bf16[256,1792]{1,0:T(8,128)(2,1)S(1)}, bf16[256,1792]{1,0:T(8,128)(2,1)}, u32[]{:S(2)}) copy-start(bf16[256,1792]{1,0:T(8,128)(2,1)} %param.8) | copy-start | bytes 2752516
  73.6 114.0 %all-gather.5.cloned.1.call-start = ((), (), s32[]{:S(2)}) async-start(), calls=%async_computation.6 | async-start | bytes 4587520 | tf_op jit(solution)/shard_map/all_gather | solution.py:32
Sparse Core Ops, SparseCore 0:
  18.3 42.0 all-gather.2
  67.7 39.8 reduce-scatter.4
  110.9 41.2 reduce-scatter.2
  156.1 31.5 all-gather.4
where the time goes:
time: 217 us
  waiting for transfers between devices  142 us (65%)
  local copies, waits for them, and re-layouts  25.9 us (12%)
  matrix products  21.8 us (10%)
  between operations  13.8 us (6%)
  blocking collectives  8.99 us (4%)
  other arithmetic  3.83 us (2%)
    reduce_scatter x2, waiting for transfers between devices, summed(): lax.psum_scatter(part.astype(jnp.bfloat16), 'fsdp', scatter_dimension=0,...  78.5 us
    all_gather x1, waiting for transfers between devices, body(): whole = lax.all_gather(pieces, 'tp', axis=1, tiled=True).reshape(-1, rows)  42.2 us
    unnamed x12, local copies, waits for them, and re-layouts  22.4 us
    all_gather x1, waiting for transfers between devices, body(): every = lax.all_gather(weighted, 'fsdp', axis=0, tiled=True)  21.7 us
    dot_general x1, matrix products, body(): lax.dot_general(whole, every, (((0,), (0,)), ((), ())), preferred_element...  11.4 us
    dot_general x2, matrix products, summed(): part = jnp.dot(whole, weight, preferred_element_type=jnp.float32)  10.4 us
    all_to_all x1, blocking collectives, body(): pieces = lax.all_to_all(pieces, 'fsdp', 0, 0, tiled=True)  8.99 us
  transfers between devices with their start and end apart: 4, of which 4 were waited for; matrix products, arithmetic and copies ran while one was open for 7% of the time, Pallas kernels for 0%

commit v1 on v0

--- a/solution.py
+++ b/solution.py
@@ -1,7 +1,347 @@
 import jax
 import jax.numpy as jnp
 from jax import lax
+from jax.experimental import pallas as pl
+from jax.experimental.pallas import tpu as pltpu
 from jax.sharding import PartitionSpec as P
+
+MESH = pl.DeviceIdType.MESH
+TILE = 256
+
+
+def pick(z, row):
+    out = row[0]
+    for index in range(1, len(row)):
+        out = jnp.where(z == index, row[index], out)
+    return out
+
+
+def kernel(
+    tokens, cotangent, up_branch, gate_weight, probe, hvp,
+    weights, tok, toks2, tok_t, psend, precv, pown, wall, cot, up,
+    own_sem, cu_sem, wl_sem, ws_sem, wr_sem, tr_sem, tx_sem, ty_sem, tu_sem, td_sem,
+    ss_sem, sr_sem, ps_sem, pr_sem, vx_sem, vs_sem, vf_sem, rx_sem, rs_sem, rf_sem,
+):
+    f = lax.axis_index("fsdp")
+    t = lax.axis_index("tp")
+    x, c, z, y = f // 2, f % 2, t // 2, t % 2
+    across = (2 * (1 - x) + c, t)
+    sibling = (2 * x + 1 - c, t)
+    beside = (f, 2 * z + 1 - y)
+    above = (f, 2 * jnp.minimum(z + 1, 3) + y)
+    below = (f, 2 * jnp.maximum(z - 1, 0) + y)
+    rows, half = gate_weight.shape[0], 2 * gate_weight.shape[0]
+    tiles = gate_weight.shape[1] // TILE
+    total_tokens = 4 * cotangent.shape[0]
+    part = 2 * tokens.shape[0]
+
+    def remote(src, dst, send, recv, device):
+        return pltpu.make_async_remote_copy(
+            src_ref=src, dst_ref=dst, send_sem=send, recv_sem=recv,
+            device_id=device, device_id_type=MESH,
+        )
+
+    def columns(index):
+        return pl.ds(pl.multiple_of(index * TILE, TILE), TILE)
+
+    own = pltpu.make_async_copy(
+        tokens.at[:, pl.ds(pl.multiple_of(x * half, 128), half)], tok.at[x, z, y], own_sem
+    )
+    own.start()
+
+    def local_weight(j, a):
+        src = (gate_weight, probe)[a]
+        return pltpu.make_async_copy(
+            src.at[:, columns(j)], weights.at[j, a, c], wl_sem.at[j, a]
+        )
+
+    @pl.loop(0, tiles)
+    def _(j):
+        for a in range(2):
+            local_weight(j, a).start()
+
+    cot_copy = pltpu.make_async_copy(cotangent, cot, cu_sem.at[0])
+    up_copy = pltpu.make_async_copy(up_branch, up, cu_sem.at[1])
+    cot_copy.start()
+    up_copy.start()
+
+    barrier = pltpu.get_barrier_semaphore()
+    for device in (across, sibling, beside):
+        pl.semaphore_signal(barrier, inc=1, device_id=device, device_id_type=MESH)
+
+    @pl.when(z < 3)
+    def _():
+        pl.semaphore_signal(barrier, inc=1, device_id=above, device_id_type=MESH)
+
+    @pl.when(z > 0)
+    def _():
+        pl.semaphore_signal(barrier, inc=1, device_id=below, device_id_type=MESH)
+
+    peers = 3 + jnp.minimum(z, 1) + jnp.minimum(3 - z, 1)
+    pl.semaphore_wait(barrier, peers)
+
+    def token_copy(xs, zs, sems, device):
+        slot = tok.at[xs, zs, y]
+        return remote(slot, slot, sems.at[xs, zs], tr_sem.at[xs, zs, y], device)
+
+    def forward_up(xs, zs):
+        @pl.when(z < 3)
+        def _():
+            token_copy(xs, zs, tu_sem, above).start()
+
+    def forward_down(xs, zs):
+        @pl.when(z > 0)
+        def _():
+            token_copy(xs, zs, td_sem, below).start()
+
+    def token_wait(xs, zs, ys):
+        slot = tok.at[xs, zs, ys]
+        remote(slot, slot, ty_sem.at[xs, zs], tr_sem.at[xs, zs, ys], beside).wait_recv()
+
+    to_across = remote(
+        tokens.at[:, pl.ds(pl.multiple_of((1 - x) * half, 128), half)],
+        tok.at[x, z, y], tx_sem, tr_sem.at[x, z, y], across,
+    )
+    to_across.start()
+    own.wait()
+    forward_up(x, z)
+    forward_down(x, z)
+    token_copy(x, z, ty_sem, beside).start()
+
+    def sibling_weight(j, a):
+        src = (gate_weight, probe)[a]
+        return remote(
+            src.at[:, columns(j)], weights.at[j, a, c], ws_sem.at[j, a], wr_sem.at[j, a], sibling
+        )
+
+    def arrived_weight(j, a):
+        slot = weights.at[j, a, 1 - c]
+        return remote(slot, slot, ws_sem.at[j, a], wr_sem.at[j, a], sibling)
+
+    @pl.loop(0, tiles)
+    def _(j):
+        for a in range(2):
+            sibling_weight(j, a).start()
+
+    token_wait(1 - x, z, y)
+    forward_up(1 - x, z)
+    forward_down(1 - x, z)
+    token_copy(1 - x, z, ty_sem, beside).start()
+
+    def forward(d):
+        @pl.when(z - d >= 0)
+        def _():
+            for xs in (x, 1 - x):
+                token_wait(xs, z - d, y)
+                forward_up(xs, z - d)
+                token_copy(xs, z - d, ty_sem, beside).start()
+
+        @pl.when(z + d <= 3)
+        def _():
+            for xs in (x, 1 - x):
+                token_wait(xs, z + d, y)
+                forward_down(xs, z + d)
+                token_copy(xs, z + d, ty_sem, beside).start()
+
+    def place(k):
+        order = ((0, 1, 2, 3), (1, 0, 2, 3), (2, 1, 3, 0), (3, 2, 1, 0))
+        return pick(z, [pick(k, line) for line in order])
+
+    def partial_copy(zk, j):
+        return remote(
+            psend.at[zk, j], precv.at[zk, j], ps_sem.at[zk, j], pr_sem.at[zk, j], across
+        )
+
+    def sibling_tokens(xs, zk):
+        return remote(
+            tok.at[xs, zk, :, :, pl.ds(pl.multiple_of((1 - c) * rows, 128), rows)],
+            toks2.at[xs, zk], ss_sem.at[xs, zk], sr_sem.at[xs, zk], sibling,
+        )
+
+    @pl.loop(0, 4)
+    def _(k):
+        zk = place(k)
+        for xs in (x, 1 - x):
+            token_wait(xs, zk, 1 - y)
+
+        @pl.loop(0, tiles)
+        def _(j):
+            @pl.when(jnp.logical_and(k < 3, j == 1))
+            def _():
+                forward(k + 1)
+
+            @pl.when(k == 0)
+            def _():
+                for a in range(2):
+                    local_weight(j, a).wait()
+                    arrived_weight(j, a).wait_recv()
+
+            lhs = jnp.concatenate(
+                [tok[1 - x, zk].reshape(part, half), tok[x, zk].reshape(part, half)], axis=0
+            )
+            for a in range(2):
+                value = jnp.dot(
+                    lhs[:, :rows], weights[j, a, 0], preferred_element_type=jnp.float32
+                ) + jnp.dot(
+                    lhs[:, rows:], weights[j, a, 1], preferred_element_type=jnp.float32
+                )
+                psend[zk, j, a] = value[:part].astype(jnp.bfloat16)
+                pown[zk, j, a] = value[part:]
+            partial_copy(zk, j).start()
+
+        for xs in range(2):
+            sibling_tokens(xs, zk).start()
+
+    cot_copy.wait()
+    up_copy.wait()
+
+    def weighted_copy(xs, zk, j, send, recv, device):
+        slot = wall.at[xs, c, zk, j]
+        return remote(slot, slot, send.at[zk, j], recv.at[zk, j], device)
+
+    @pl.loop(0, 4)
+    def _(k):
+        zk = place(k)
+
+        @pl.loop(0, tiles)
+        def _(j):
+            partial_copy(zk, j).wait_recv()
+            gate = pown[zk, j, 0] + precv[zk, j, 0].astype(jnp.float32)
+            tangent = pown[zk, j, 1] + precv[zk, j, 1].astype(jnp.float32)
+            sig = jax.nn.sigmoid(gate)
+            second = sig * (1.0 - sig) * (2.0 + gate * (1.0 - 2.0 * sig))
+            lines = pl.ds(pl.multiple_of(zk * part, part), part)
+            wall[x, c, zk, j] = (
+                cot[lines, columns(j)].astype(jnp.float32)
+                * up[lines, columns(j)].astype(jnp.float32)
+                * second
+                * tangent
+                * (1.0 / total_tokens)
+            ).astype(jnp.bfloat16)
+            weighted_copy(x, zk, j, vx_sem, rx_sem, across).start()
+            weighted_copy(x, zk, j, vs_sem, rs_sem, sibling).start()
+
+        mine = pl.ds(pl.multiple_of(c * rows, 128), rows)
+        for xs in range(2):
+            remote(
+                toks2.at[xs, zk], toks2.at[xs, zk], ss_sem.at[xs, zk], sr_sem.at[xs, zk], sibling
+            ).wait_recv()
+        lines = [tok[xs, zk, :, :, mine].reshape(part, rows) for xs in range(2)]
+        lines += [toks2[xs, zk].reshape(part, rows) for xs in range(2)]
+        whole = jnp.concatenate(lines, axis=0).astype(jnp.float32)
+        tok_t[k] = whole.T.astype(jnp.bfloat16)
+
+    def arrived(xs, zk, j, recv):
+        slot = wall.at[xs, 1 - c, zk, j]
+        return remote(slot, slot, vs_sem.at[zk, j], recv.at[zk, j], sibling)
+
+    def pass_on(k):
+        zk = place(k)
+
+        @pl.loop(0, tiles)
+        def _(j):
+            slot = wall.at[1 - x, c, zk, j]
+            remote(slot, slot, vx_sem.at[zk, j], rx_sem.at[zk, j], across).wait_recv()
+            weighted_copy(1 - x, zk, j, vf_sem, rf_sem, sibling).start()
+
+    def backward(k):
+        zk = place(k)
+
+        @pl.loop(0, tiles)
+        def _(j):
+            arrived(x, zk, j, rs_sem).wait_recv()
+            arrived(1 - x, zk, j, rf_sem).wait_recv()
+            rhs = jnp.concatenate(
+                [wall[0, c, zk, j], wall[1, c, zk, j], wall[0, 1 - c, zk, j], wall[1, 1 - c, zk, j]],
+                axis=0,
+            )
+            value = jnp.dot(tok_t[k], rhs, preferred_element_type=jnp.float32)
+
+            @pl.when(k == 0)
+            def _():
+                hvp[:, columns(j)] = value
+
+            @pl.when(k > 0)
+            def _():
+                hvp[:, columns(j)] += value
+
+    @pl.loop(0, 5)
+    def _(k):
+        @pl.when(k < 4)
+        def _():
+            pass_on(k)
+
+        @pl.when(k > 0)
+        def _():
+            backward(k - 1)
+
+    to_across.wait_send()
+
+    @pl.loop(0, tiles)
+    def _(j):
+        for a in range(2):
+            sibling_weight(j, a).wait_send()
+
+    @pl.loop(0, 4)
+    def _(zk):
+        for xs in range(2):
+            token_copy(xs, zk, ty_sem, beside).wait_send()
+            sibling_tokens(xs, zk).wait_send()
+
+            @pl.when(jnp.logical_and(z < 3, zk <= z))
+            def _():
+                token_copy(xs, zk, tu_sem, above).wait_send()
+
+            @pl.when(jnp.logical_and(z > 0, zk >= z))
+            def _():
+                token_copy(xs, zk, td_sem, below).wait_send()
+
+        @pl.loop(0, tiles)
+        def _(j):
+            partial_copy(zk, j).wait_send()
+            weighted_copy(x, zk, j, vx_sem, rx_sem, across).wait_send()
+            weighted_copy(x, zk, j, vs_sem, rs_sem, sibling).wait_send()
+            weighted_copy(1 - x, zk, j, vf_sem, rf_sem, sibling).wait_send()
+
+
+def small_body(tokens, cotangent, up_branch, gate_weight, probe, hess_ema):
+    rows, width = gate_weight.shape
+    lines = tokens.shape[0]
+    part, tiles = 2 * lines, width // TILE
+    bf16, f32, dma = jnp.bfloat16, jnp.float32, pltpu.SemaphoreType.DMA
+    anywhere = pl.BlockSpec(memory_space=pl.ANY)
+    grid = (4, tiles)
+    hvp = pl.pallas_call(
+        kernel,
+        out_shape=jax.ShapeDtypeStruct((rows, width), f32),
+        in_specs=[anywhere] * 5,
+        out_specs=pl.BlockSpec(memory_space=pltpu.VMEM),
+        scratch_shapes=[
+            pltpu.VMEM((tiles, 2, 2, rows, TILE), bf16),
+            pltpu.VMEM((2, 4, 2, lines, 2 * rows), bf16),
+            pltpu.VMEM((2, 4, 2, lines, rows), bf16),
+            pltpu.VMEM((4, rows, 4 * part), bf16),
+            pltpu.VMEM((4, tiles, 2, part, TILE), bf16),
+            pltpu.VMEM((4, tiles, 2, part, TILE), bf16),
+            pltpu.VMEM((4, tiles, 2, part, TILE), f32),
+            pltpu.VMEM((2, 2, 4, tiles, part, TILE), bf16),
+            pltpu.VMEM(cotangent.shape, bf16),
+            pltpu.VMEM(up_branch.shape, bf16),
+            dma, dma((2,)), dma((tiles, 2)), dma((tiles, 2)), dma((tiles, 2)),
+            dma((2, 4, 2)), dma, dma((2, 4)), dma((2, 4)), dma((2, 4)),
+            dma((2, 4)), dma((2, 4)), dma(grid), dma(grid),
+            dma(grid), dma(grid), dma(grid), dma(grid), dma(grid), dma(grid),
+        ],
+        compiler_params=pltpu.CompilerParams(
+            collective_id=0, has_side_effects=True, vmem_limit_bytes=44 * 1024 * 1024
+        ),
+        cost_estimate=pl.CostEstimate(
+            flops=7_000_000_000, bytes_accessed=12_000_000, transcendentals=500_000
+        ),
+    )(tokens, cotangent, up_branch, gate_weight, probe)
+    hess_diag = probe.astype(f32) * hvp
+    ema_next = 0.99 * hess_ema + 0.01 * hess_diag
+    return (hess_diag, ema_next)
 
 
 def body(tokens, cotangent, up_branch, gate_weight, probe, hess_ema):
@@ -47,8 +387,9 @@
         P("fsdp", "tp"),
         P("fsdp", "tp"),
     )
+    small = mesh.shape["fsdp"] == 4 and mesh.shape["tp"] == 8
     return jax.shard_map(
-        body,
+        small_body if small else body,
         mesh=mesh,
         in_specs=placed,
         out_specs=(P("fsdp", "tp"), P("fsdp", "tp")),

time: 217 us -> 94.6 us (0.44)
  waiting for transfers between devices: 142 us -> 0 us
  Pallas kernels: 0 us -> 80.2 us
  matrix products: 21.8 us -> 0 us
  local copies, waits for them, and re-layouts: 25.9 us -> 6.57 us
  between operations: 13.8 us -> 0.67 us
  blocking collectives: 8.99 us -> 0 us
  other arithmetic: 3.83 us -> 6.84 us
    pallas_call x0 -> x1, Pallas kernels: none -> 80.2 us  [small_body(): pl.pallas_call(kernel, out_shape=jax.ShapeDtypeStruct((rows, width), f32)...]
    reduce_scatter x2 -> x0, waiting for transfers between devices: 78.5 us -> none  [summed(): lax.psum_scatter(part.astype(jnp.bfloat16), 'fsdp', scatter_dimension=0,...]
    all_gather x2 -> x0, waiting for transfers between devices: 63.9 us -> none  [the longest x1 42.2 us: body(): whole = lax.all_gather(pieces, 'tp', axis=1, tiled=True).reshape(-1, rows)]
    dot_general x3 -> x0, matrix products: 21.8 us -> none  [the longest x1 11.4 us: body(): lax.dot_general(whole, every, (((0,), (0,)), ((), ())), preferred_element...]
    unnamed x12 -> x14, local copies, waits for them, and re-layouts: 22.4 us -> 6.57 us
    all_to_all x1 -> x0, blocking collectives: 8.99 us -> none  [body(): pieces = lax.all_to_all(pieces, 'fsdp', 0, 0, tiled=True)]
    add x0 -> x1, other arithmetic: none -> 6.84 us  [small_body(): ema_next = 0.99 * hess_ema + 0.01 * hess_diag]
    convert_element_type x1 -> x0, other arithmetic: 3.83 us -> none  [body(): weighted = (cotangent.astype(jnp.float32) * up_branch.astype(jnp.float32)...]
  transfers between devices with their start and end apart: 4 -> 0, of which waited for: 4 -> 0; matrix products, arithmetic and copies ran while one was open for 7% -> 0% of each run, Pallas kernels for 0% -> 0%
where the time goes in v1:
time: 94.6 us; the launch traced here: 94.2 us
  Pallas kernels  80.2 us (85%)
  other arithmetic  6.84 us (7%)
  local copies, waits for them, and re-layouts  6.57 us (7%)
    pallas_call x1, Pallas kernels, small_body(): pl.pallas_call(kernel, out_shape=jax.ShapeDtypeStruct((rows, width), f32)...  80.2 us
    add x1, other arithmetic, small_body(): ema_next = 0.99 * hess_ema + 0.01 * hess_diag  6.84 us
    unnamed x14, local copies, waits for them, and re-layouts  6.57 us

profile of v1, /device:TPU:0, one launch (start us, length us, event | category | flops | bytes accessed | tf_op | source)
XLA Modules:
  0.0 94.2 jit_solution(12254478762983694704)
XLA Ops:
  0.6 0.0 copy-start
  0.6 1.6 %copy-done = bf16[640,1792]{1,0:T(8,128)(2,1)S(1)} copy-done((bf16[640,1792]{1,0:T(8,128)(2,1)S(1)}, bf16[640,1792]{1,0:T(8,128)(2,1)}, u32[]{:S(2)}) %copy-start) | copy-done | bytes 2293784
  2.3 0.0 copy-start.2
  2.3 1.6 %copy-done.2 = bf16[640,1792]{1,0:T(8,128)(2,1)S(1)} copy-done((bf16[640,1792]{1,0:T(8,128)(2,1)S(1)}, bf16[640,1792]{1,0:T(8,128)(2,1)}, u32[]{:S(2)}) %copy-start.2) | copy-done | bytes 2293784
  3.9 0.0 copy-start.3
  3.9 1.2 %copy-done.3 = bf16[256,1792]{1,0:T(8,128)(2,1)S(1)} copy-done((bf16[256,1792]{1,0:T(8,128)(2,1)S(1)}, bf16[256,1792]{1,0:T(8,128)(2,1)}, u32[]{:S(2)}) %copy-start.3) | copy-done | bytes 917528
  5.1 0.0 copy-start.4
  5.1 1.2 %copy-done.4 = bf16[256,1792]{1,0:T(8,128)(2,1)S(1)} copy-done((bf16[256,1792]{1,0:T(8,128)(2,1)S(1)}, bf16[256,1792]{1,0:T(8,128)(2,1)}, u32[]{:S(2)}) %copy-start.4) | copy-done | bytes 917528
  6.3 0.0 copy-start.5
  6.3 0.9 copy-done.5
  7.2 0.0 copy-start.1
  7.2 0.0 copy-start.6
  7.2 80.2 %shard_map.77 = f32[640,1792]{1,0:T(8,128)} custom-call(bf16[32,2560]{1,0:T(8,128)(2,1)S(1)} %copy-done.5, bf16[256,1792]{1,0:T(8,128)(2,1)S(1)} %copy-done.3, bf16[256,1792]{1,0:T(8,128)(2,1)S(1)} %copy-done.4, bf16[640,1792]{1,0:T(8,128)(2,1)S(1)} %copy-done.2, bf16[640,1792]{1,0:T(8,128)(2,1)S(1)} %copy-done), custom_call_target="tpu_custom_call" | custom-call | flops 7000000000 | bytes 12000000 | tf_op jit(solution)/shard_map/pallas_call | solution.py:314
  87.4 0.0 copy-done.1
  87.4 0.0 copy-done.6
  87.4 6.8 %multiply_add_fusion = (f32[640,1792]{1,0:T(8,128)}, f32[640,1792]{1,0:T(8,128)}) fusion(f32[640,1792]{1,0:T(8,128)S(1)} %copy-done.6, f32[640,1792]{1,0:T(8,128)} %shard_map.77, bf16[640,1792]{1,0:T(8,128)(2,1)S(1)} %copy-done.1), kind=kLoop, calls=%fused_computation | loop fusion | flops 5734400 | bytes 20643840 | tf_op jit(solution)/shard_map/add | solution.py:343
Async XLA Ops:
  0.6 1.6 %copy-start = (bf16[640,1792]{1,0:T(8,128)(2,1)S(1)}, bf16[640,1792]{1,0:T(8,128)(2,1)}, u32[]{:S(2)}) copy-start(bf16[640,1792]{1,0:T(8,128)(2,1)} %probe.1) | copy-start | bytes 6881284
  2.3 1.6 %copy-start.2 = (bf16[640,1792]{1,0:T(8,128)(2,1)S(1)}, bf16[640,1792]{1,0:T(8,128)(2,1)}, u32[]{:S(2)}) copy-start(bf16[640,1792]{1,0:T(8,128)(2,1)} %gate_weight.1) | copy-start | bytes 6881284
  3.9 1.2 %copy-start.3 = (bf16[256,1792]{1,0:T(8,128)(2,1)S(1)}, bf16[256,1792]{1,0:T(8,128)(2,1)}, u32[]{:S(2)}) copy-start(bf16[256,1792]{1,0:T(8,128)(2,1)} %cotangent.1) | copy-start | bytes 2752516
  5.1 1.2 %copy-start.4 = (bf16[256,1792]{1,0:T(8,128)(2,1)S(1)}, bf16[256,1792]{1,0:T(8,128)(2,1)}, u32[]{:S(2)}) copy-start(bf16[256,1792]{1,0:T(8,128)(2,1)} %up_branch.1) | copy-start | bytes 2752516
  6.3 0.9 copy-start.5
  7.2 80.2 %copy-start.1 = (bf16[640,1792]{1,0:T(8,128)(2,1)S(1)}, bf16[640,1792]{1,0:T(8,128)(2,1)}, u32[]{:S(2)}) copy-start(bf16[640,1792]{1,0:T(8,128)(2,1)} %probe.1) | copy-start | bytes 6881284
  7.2 80.2 %copy-start.6 = (f32[640,1792]{1,0:T(8,128)S(1)}, f32[640,1792]{1,0:T(8,128)}, u32[]{:S(2)}) copy-start(f32[640,1792]{1,0:T(8,128)} %param.11) | copy-start | bytes 13762564

commit v2 on v1

--- a/solution.py
+++ b/solution.py
@@ -309,11 +309,11 @@
     lines = tokens.shape[0]
     part, tiles = 2 * lines, width // TILE
     bf16, f32, dma = jnp.bfloat16, jnp.float32, pltpu.SemaphoreType.DMA
-    anywhere = pl.BlockSpec(memory_space=pl.ANY)
+    anywhere = pl.BlockSpec(memory_space=pltpu.HBM)
     grid = (4, tiles)
     hvp = pl.pallas_call(
         kernel,
-        out_shape=jax.ShapeDtypeStruct((rows, width), f32),
+        out_shape=pltpu.VMEM((rows, width), f32),
         in_specs=[anywhere] * 5,
         out_specs=pl.BlockSpec(memory_space=pltpu.VMEM),
         scratch_shapes=[
@@ -338,7 +338,10 @@
         cost_estimate=pl.CostEstimate(
             flops=7_000_000_000, bytes_accessed=12_000_000, transcendentals=500_000
         ),
-    )(tokens, cotangent, up_branch, gate_weight, probe)
+    )(*(
+        pltpu.with_memory_space_constraint(operand, pltpu.HBM)
+        for operand in (tokens, cotangent, up_branch, gate_weight, probe)
+    ))
     hess_diag = probe.astype(f32) * hvp
     ema_next = 0.99 * hess_ema + 0.01 * hess_diag
     return (hess_diag, ema_next)

time: 94.6 us -> 83 us (0.88)
  local copies, waits for them, and re-layouts: 6.57 us -> 0.01 us
  Pallas kernels: 80.2 us -> 77.6 us
  other arithmetic: 6.84 us -> 4.54 us
    unnamed x14 -> x4, local copies, waits for them, and re-layouts: 6.57 us -> 0.01 us
    pallas_call x1, Pallas kernels: 80.2 us -> 77.6 us  [small_body(): pl.pallas_call(kernel, out_shape=pltpu.VMEM((rows, width), f32), in_specs...]
    add x1, other arithmetic: 6.84 us -> 4.54 us  [small_body(): ema_next = 0.99 * hess_ema + 0.01 * hess_diag]
where the time goes in v2:
time: 83 us; the launch traced here: 82.8 us
  Pallas kernels  77.6 us (93%)
  other arithmetic  4.54 us (5%)
    pallas_call x1, Pallas kernels, small_body(): pl.pallas_call(kernel, out_shape=pltpu.VMEM((rows, width), f32), in_specs...  77.6 us
    add x1, other arithmetic, small_body(): ema_next = 0.99 * hess_ema + 0.01 * hess_diag  4.54 us

profile of v2, /device:TPU:0, one launch (start us, length us, event | category | flops | bytes accessed | tf_op | source)
XLA Modules:
  0.0 82.8 jit_solution(6238217864423884056)
XLA Ops:
  0.6 0.0 copy-start.1
  0.6 0.0 copy-start
  0.7 77.6 %shard_map.77 = f32[640,1792]{1,0:T(8,128)S(1)} custom-call(bf16[32,2560]{1,0:T(8,128)(2,1)} %tokens.1, bf16[256,1792]{1,0:T(8,128)(2,1)} %cotangent.1, bf16[256,1792]{1,0:T(8,128)(2,1)} %up_branch.1, bf16[640,1792]{1,0:T(8,128)(2,1)} %gate_weight.1, bf16[640,1792]{1,0:T(8,128)(2,1)} %probe.1), custom_call_target="tpu_custom_call" | custom-call | flops 7000000000 | bytes 12000000 | tf_op jit(solution)/shard_map/pallas_call | solution.py:314
  78.3 0.0 copy-done.1
  78.3 0.0 copy-done
  78.3 4.5 %multiply_add_fusion = (f32[640,1792]{1,0:T(8,128)}, f32[640,1792]{1,0:T(8,128)}) fusion(f32[640,1792]{1,0:T(8,128)S(1)} %copy-done, f32[640,1792]{1,0:T(8,128)S(1)} %shard_map.77, bf16[640,1792]{1,0:T(8,128)(2,1)S(1)} %copy-done.1), kind=kLoop, calls=%fused_computation | loop fusion | flops 5734400 | bytes 20643840 | tf_op jit(solution)/shard_map/add | solution.py:346
Async XLA Ops:
  0.6 77.6 %copy-start.1 = (bf16[640,1792]{1,0:T(8,128)(2,1)S(1)}, bf16[640,1792]{1,0:T(8,128)(2,1)}, u32[]{:S(2)}) copy-start(bf16[640,1792]{1,0:T(8,128)(2,1)} %probe.1) | copy-start | bytes 6881284
  0.6 77.6 %copy-start = (f32[640,1792]{1,0:T(8,128)S(1)}, f32[640,1792]{1,0:T(8,128)}, u32[]{:S(2)}) copy-start(f32[640,1792]{1,0:T(8,128)} %param.11) | copy-start | bytes 13762564

commit v3 on v2

--- a/solution.py
+++ b/solution.py
@@ -20,7 +20,7 @@
     tokens, cotangent, up_branch, gate_weight, probe, hvp,
     weights, tok, toks2, tok_t, psend, precv, pown, wall, cot, up,
     own_sem, cu_sem, wl_sem, ws_sem, wr_sem, tr_sem, tx_sem, ty_sem, tu_sem, td_sem,
-    ss_sem, sr_sem, ps_sem, pr_sem, vx_sem, vs_sem, vf_sem, rx_sem, rs_sem, rf_sem,
+    ss_sem, sr_sem, ps_sem, pr_sem, vx_sem, vs_sem, vf_sem, rx_sem, rs_sem, rf_sem, fs_sem, fr_sem,
 ):
     f = lax.axis_index("fsdp")
     t = lax.axis_index("tp")
@@ -103,26 +103,27 @@
         tok.at[x, z, y], tx_sem, tr_sem.at[x, z, y], across,
     )
     to_across.start()
+
+    def sibling_weight(j, a):
+        src = (gate_weight, probe)[a]
+        return remote(
+            src.at[:, columns(j)], weights.at[j, a, c], ws_sem.at[j, a], wr_sem.at[j, a], sibling
+        )
+
+    def arrived_weight(j, a):
+        slot = weights.at[j, a, 1 - c]
+        return remote(slot, slot, ws_sem.at[j, a], wr_sem.at[j, a], sibling)
+
+    @pl.loop(0, tiles)
+    def _(j):
+        for a in range(2):
+            sibling_weight(j, a).start()
+
     own.wait()
     forward_up(x, z)
     forward_down(x, z)
     token_copy(x, z, ty_sem, beside).start()
 
-    def sibling_weight(j, a):
-        src = (gate_weight, probe)[a]
-        return remote(
-            src.at[:, columns(j)], weights.at[j, a, c], ws_sem.at[j, a], wr_sem.at[j, a], sibling
-        )
-
-    def arrived_weight(j, a):
-        slot = weights.at[j, a, 1 - c]
-        return remote(slot, slot, ws_sem.at[j, a], wr_sem.at[j, a], sibling)
-
-    @pl.loop(0, tiles)
-    def _(j):
-        for a in range(2):
-            sibling_weight(j, a).start()
-
     token_wait(1 - x, z, y)
     forward_up(1 - x, z)
     forward_down(1 - x, z)
@@ -158,9 +159,55 @@
             toks2.at[xs, zk], ss_sem.at[xs, zk], sr_sem.at[xs, zk], sibling,
         )
 
-    @pl.loop(0, 4)
+    def product(lhs, j, a):
+        return jnp.dot(
+            lhs[:, :rows], weights[j, a, 0], preferred_element_type=jnp.float32
+        ) + jnp.dot(lhs[:, rows:], weights[j, a, 1], preferred_element_type=jnp.float32)
+
+    lines = part // 2
+
+    def first_copy(ys, j):
+        band = pl.ds(pl.multiple_of(ys * lines, lines), lines)
+        return remote(
+            psend.at[z, j, :, band], precv.at[z, j, :, band],
+            fs_sem.at[ys, j], fr_sem.at[ys, j], across,
+        )
+
+    def first_half(ys, j):
+        lhs = jnp.concatenate([tok[1 - x, z, ys], tok[x, z, ys]], axis=0)
+        band = pl.ds(pl.multiple_of(ys * lines, lines), lines)
+        for a in range(2):
+            value = product(lhs, j, a)
+            psend[z, j, a, band, :] = value[:lines].astype(jnp.bfloat16)
+            pown[z, j, a, band, :] = value[lines:]
+        first_copy(ys, j).start()
+
+    @pl.loop(0, tiles + 2)
+    def _(j):
+        @pl.when(j < tiles)
+        def _():
+            for a in range(2):
+                local_weight(j, a).wait()
+                arrived_weight(j, a).wait_recv()
+            first_half(y, j)
+
+        @pl.when(j == 1)
+        def _():
+            forward(1)
+            for xs in (x, 1 - x):
+                token_wait(xs, z, 1 - y)
+
+        @pl.when(j >= 2)
+        def _():
+            first_half(1 - y, j - 2)
+
+    for xs in range(2):
+        sibling_tokens(xs, z).start()
+
+    @pl.loop(1, 4)
     def _(k):
         zk = place(k)
+
         for xs in (x, 1 - x):
             token_wait(xs, zk, 1 - y)
 
@@ -170,21 +217,11 @@
             def _():
                 forward(k + 1)
 
-            @pl.when(k == 0)
-            def _():
-                for a in range(2):
-                    local_weight(j, a).wait()
-                    arrived_weight(j, a).wait_recv()
-
             lhs = jnp.concatenate(
                 [tok[1 - x, zk].reshape(part, half), tok[x, zk].reshape(part, half)], axis=0
             )
             for a in range(2):
-                value = jnp.dot(
-                    lhs[:, :rows], weights[j, a, 0], preferred_element_type=jnp.float32
-                ) + jnp.dot(
-                    lhs[:, rows:], weights[j, a, 1], preferred_element_type=jnp.float32
-                )
+                value = product(lhs, j, a)
                 psend[zk, j, a] = value[:part].astype(jnp.bfloat16)
                 pown[zk, j, a] = value[part:]
             partial_copy(zk, j).start()
@@ -205,7 +242,15 @@
 
         @pl.loop(0, tiles)
         def _(j):
-            partial_copy(zk, j).wait_recv()
+            @pl.when(k == 0)
+            def _():
+                for ys in range(2):
+                    first_copy(ys, j).wait_recv()
+
+            @pl.when(k > 0)
+            def _():
+                partial_copy(zk, j).wait_recv()
+
             gate = pown[zk, j, 0] + precv[zk, j, 0].astype(jnp.float32)
             tangent = pown[zk, j, 1] + precv[zk, j, 1].astype(jnp.float32)
             sig = jax.nn.sigmoid(gate)
@@ -235,45 +280,42 @@
         slot = wall.at[xs, 1 - c, zk, j]
         return remote(slot, slot, vs_sem.at[zk, j], recv.at[zk, j], sibling)
 
-    def pass_on(k):
+    def pass_on(k, j):
         zk = place(k)
-
-        @pl.loop(0, tiles)
-        def _(j):
-            slot = wall.at[1 - x, c, zk, j]
-            remote(slot, slot, vx_sem.at[zk, j], rx_sem.at[zk, j], across).wait_recv()
-            weighted_copy(1 - x, zk, j, vf_sem, rf_sem, sibling).start()
-
-    def backward(k):
+        slot = wall.at[1 - x, c, zk, j]
+        remote(slot, slot, vx_sem.at[zk, j], rx_sem.at[zk, j], across).wait_recv()
+        weighted_copy(1 - x, zk, j, vf_sem, rf_sem, sibling).start()
+
+    def backward(k, j):
         zk = place(k)
-
-        @pl.loop(0, tiles)
-        def _(j):
-            arrived(x, zk, j, rs_sem).wait_recv()
-            arrived(1 - x, zk, j, rf_sem).wait_recv()
-            rhs = jnp.concatenate(
-                [wall[0, c, zk, j], wall[1, c, zk, j], wall[0, 1 - c, zk, j], wall[1, 1 - c, zk, j]],
-                axis=0,
-            )
-            value = jnp.dot(tok_t[k], rhs, preferred_element_type=jnp.float32)
-
-            @pl.when(k == 0)
-            def _():
-                hvp[:, columns(j)] = value
-
-            @pl.when(k > 0)
-            def _():
-                hvp[:, columns(j)] += value
-
-    @pl.loop(0, 5)
-    def _(k):
-        @pl.when(k < 4)
-        def _():
-            pass_on(k)
+        arrived(x, zk, j, rs_sem).wait_recv()
+        arrived(1 - x, zk, j, rf_sem).wait_recv()
+        rhs = jnp.concatenate(
+            [wall[0, c, zk, j], wall[1, c, zk, j], wall[0, 1 - c, zk, j], wall[1, 1 - c, zk, j]],
+            axis=0,
+        )
+        value = jnp.dot(tok_t[k], rhs, preferred_element_type=jnp.float32)
+
+        @pl.when(k == 0)
+        def _():
+            hvp[:, columns(j)] = value
 
         @pl.when(k > 0)
         def _():
-            backward(k - 1)
+            hvp[:, columns(j)] += value
+
+        @pl.when(k == 0)
+        def _():
+            for ys in range(2):
+                first_copy(ys, j).wait_send()
+
+        @pl.when(k > 0)
+        def _():
+            partial_copy(zk, j).wait_send()
+
+        weighted_copy(x, zk, j, vx_sem, rx_sem, across).wait_send()
+        weighted_copy(x, zk, j, vs_sem, rs_sem, sibling).wait_send()
+        weighted_copy(1 - x, zk, j, vf_sem, rf_sem, sibling).wait_send()
 
     to_across.wait_send()
 
@@ -296,12 +338,17 @@
             def _():
                 token_copy(xs, zk, td_sem, below).wait_send()
 
-        @pl.loop(0, tiles)
-        def _(j):
-            partial_copy(zk, j).wait_send()
-            weighted_copy(x, zk, j, vx_sem, rx_sem, across).wait_send()
-            weighted_copy(x, zk, j, vs_sem, rs_sem, sibling).wait_send()
-            weighted_copy(1 - x, zk, j, vf_sem, rf_sem, sibling).wait_send()
+    lag = 2
+
+    @pl.loop(0, 4 * tiles + lag)
+    def _(u):
+        @pl.when(u < 4 * tiles)
+        def _():
+            pass_on(u // tiles, u % tiles)
+
+        @pl.when(u >= lag)
+        def _():
+            backward((u - lag) // tiles, (u - lag) % tiles)
 
 
 def small_body(tokens, cotangent, up_branch, gate_weight, probe, hess_ema):
@@ -331,6 +378,7 @@
             dma((2, 4, 2)), dma, dma((2, 4)), dma((2, 4)), dma((2, 4)),
             dma((2, 4)), dma((2, 4)), dma(grid), dma(grid),
             dma(grid), dma(grid), dma(grid), dma(grid), dma(grid), dma(grid),
+            dma((2, tiles)), dma((2, tiles)),
         ],
         compiler_params=pltpu.CompilerParams(
             collective_id=0, has_side_effects=True, vmem_limit_bytes=44 * 1024 * 1024

time: 83 us -> 79.3 us (0.955)
  Pallas kernels: 77.6 us -> 73.9 us
    pallas_call x1, Pallas kernels: 77.6 us -> 73.9 us  [small_body(): pl.pallas_call(kernel, out_shape=pltpu.VMEM((rows, width), f32), in_specs...]
where the time goes in v3:
time: 79.3 us; the launch traced here: 79.2 us
  Pallas kernels  73.9 us (93%)
  other arithmetic  4.54 us (6%)
    pallas_call x1, Pallas kernels, small_body(): pl.pallas_call(kernel, out_shape=pltpu.VMEM((rows, width), f32), in_specs...  73.9 us
    add x1, other arithmetic, small_body(): ema_next = 0.99 * hess_ema + 0.01 * hess_diag  4.54 us

profile of v3, /device:TPU:0, one launch (start us, length us, event | category | flops | bytes accessed | tf_op | source)
XLA Modules:
  0.0 79.2 jit_solution(13112434733377247076)
XLA Ops:
  0.6 0.0 copy-start.1
  0.6 0.0 copy-start
  0.7 73.9 %shard_map.77 = f32[640,1792]{1,0:T(8,128)S(1)} custom-call(bf16[32,2560]{1,0:T(8,128)(2,1)} %tokens.1, bf16[256,1792]{1,0:T(8,128)(2,1)} %cotangent.1, bf16[256,1792]{1,0:T(8,128)(2,1)} %up_branch.1, bf16[640,1792]{1,0:T(8,128)(2,1)} %gate_weight.1, bf16[640,1792]{1,0:T(8,128)(2,1)} %probe.1), custom_call_target="tpu_custom_call" | custom-call | flops 7000000000 | bytes 12000000 | tf_op jit(solution)/shard_map/pallas_call | solution.py:361
  74.6 0.0 copy-done.1
  74.6 0.0 copy-done
  74.6 4.5 %multiply_add_fusion = (f32[640,1792]{1,0:T(8,128)}, f32[640,1792]{1,0:T(8,128)}) fusion(f32[640,1792]{1,0:T(8,128)S(1)} %copy-done, f32[640,1792]{1,0:T(8,128)S(1)} %shard_map.77, bf16[640,1792]{1,0:T(8,128)(2,1)S(1)} %copy-done.1), kind=kLoop, calls=%fused_computation | loop fusion | flops 5734400 | bytes 20643840 | tf_op jit(solution)/shard_map/add | solution.py:394
Async XLA Ops:
  0.6 74.0 %copy-start.1 = (bf16[640,1792]{1,0:T(8,128)(2,1)S(1)}, bf16[640,1792]{1,0:T(8,128)(2,1)}, u32[]{:S(2)}) copy-start(bf16[640,1792]{1,0:T(8,128)(2,1)} %probe.1) | copy-start | bytes 6881284
  0.6 74.0 %copy-start = (f32[640,1792]{1,0:T(8,128)S(1)}, f32[640,1792]{1,0:T(8,128)}, u32[]{:S(2)}) copy-start(f32[640,1792]{1,0:T(8,128)} %param.11) | copy-start | bytes 13762564

commit v4 on v3

--- a/solution.py
+++ b/solution.py
@@ -338,7 +338,7 @@
             def _():
                 token_copy(xs, zk, td_sem, below).wait_send()
 
-    lag = 2
+    lag = 3
 
     @pl.loop(0, 4 * tiles + lag)
     def _(u):

time: 79.3 us -> 79 us (level)
  no operation moved by 1% of the time
where the time goes in v4:
time: 79 us; the launch traced here: 78.8 us
  Pallas kernels  73.6 us (93%)
  other arithmetic  4.54 us (6%)
    pallas_call x1, Pallas kernels, small_body(): pl.pallas_call(kernel, out_shape=pltpu.VMEM((rows, width), f32), in_specs...  73.6 us
    add x1, other arithmetic, small_body(): ema_next = 0.99 * hess_ema + 0.01 * hess_diag  4.54 us

profile of v4, /device:TPU:0, one launch (start us, length us, event | category | flops | bytes accessed | tf_op | source)
XLA Modules:
  0.0 78.8 jit_solution(4131375602069387620)
XLA Ops:
  0.6 0.0 copy-start.1
  0.6 0.0 copy-start
  0.7 73.6 %shard_map.77 = f32[640,1792]{1,0:T(8,128)S(1)} custom-call(bf16[32,2560]{1,0:T(8,128)(2,1)} %tokens.1, bf16[256,1792]{1,0:T(8,128)(2,1)} %cotangent.1, bf16[256,1792]{1,0:T(8,128)(2,1)} %up_branch.1, bf16[640,1792]{1,0:T(8,128)(2,1)} %gate_weight.1, bf16[640,1792]{1,0:T(8,128)(2,1)} %probe.1), custom_call_target="tpu_custom_call" | custom-call | flops 7000000000 | bytes 12000000 | tf_op jit(solution)/shard_map/pallas_call | solution.py:361
  74.3 0.0 copy-done.1
  74.3 0.0 copy-done
  74.3 4.5 %multiply_add_fusion = (f32[640,1792]{1,0:T(8,128)}, f32[640,1792]{1,0:T(8,128)}) fusion(f32[640,1792]{1,0:T(8,128)S(1)} %copy-done, f32[640,1792]{1,0:T(8,128)S(1)} %shard_map.77, bf16[640,1792]{1,0:T(8,128)(2,1)S(1)} %copy-done.1), kind=kLoop, calls=%fused_computation | loop fusion | flops 5734400 | bytes 20643840 | tf_op jit(solution)/shard_map/add | solution.py:394
Async XLA Ops:
  0.6 73.6 %copy-start.1 = (bf16[640,1792]{1,0:T(8,128)(2,1)S(1)}, bf16[640,1792]{1,0:T(8,128)(2,1)}, u32[]{:S(2)}) copy-start(bf16[640,1792]{1,0:T(8,128)(2,1)} %probe.1) | copy-start | bytes 6881284
  0.6 73.6 %copy-start = (f32[640,1792]{1,0:T(8,128)S(1)}, f32[640,1792]{1,0:T(8,128)}, u32[]{:S(2)}) copy-start(f32[640,1792]{1,0:T(8,128)} %param.11) | copy-start | bytes 13762564

commit v5 on v4

--- a/solution.py
+++ b/solution.py
@@ -44,6 +44,18 @@
     def columns(index):
         return pl.ds(pl.multiple_of(index * TILE, TILE), TILE)
 
+    barrier = pltpu.get_barrier_semaphore()
+    for device in (across, sibling, beside):
+        pl.semaphore_signal(barrier, inc=1, device_id=device, device_id_type=MESH)
+
+    @pl.when(z < 3)
+    def _():
+        pl.semaphore_signal(barrier, inc=1, device_id=above, device_id_type=MESH)
+
+    @pl.when(z > 0)
+    def _():
+        pl.semaphore_signal(barrier, inc=1, device_id=below, device_id_type=MESH)
+
     own = pltpu.make_async_copy(
         tokens.at[:, pl.ds(pl.multiple_of(x * half, 128), half)], tok.at[x, z, y], own_sem
     )
@@ -64,18 +76,6 @@
     up_copy = pltpu.make_async_copy(up_branch, up, cu_sem.at[1])
     cot_copy.start()
     up_copy.start()
-
-    barrier = pltpu.get_barrier_semaphore()
-    for device in (across, sibling, beside):
-        pl.semaphore_signal(barrier, inc=1, device_id=device, device_id_type=MESH)
-
-    @pl.when(z < 3)
-    def _():
-        pl.semaphore_signal(barrier, inc=1, device_id=above, device_id_type=MESH)
-
-    @pl.when(z > 0)
-    def _():
-        pl.semaphore_signal(barrier, inc=1, device_id=below, device_id_type=MESH)
 
     peers = 3 + jnp.minimum(z, 1) + jnp.minimum(3 - z, 1)
     pl.semaphore_wait(barrier, peers)

time: 79 us -> 78.9 us (level)
  no operation moved by 1% of the time
where the time goes in v5:
time: 78.9 us; the launch traced here: 78.8 us
  Pallas kernels  73.5 us (93%)
  other arithmetic  4.54 us (6%)
    pallas_call x1, Pallas kernels, small_body(): pl.pallas_call(kernel, out_shape=pltpu.VMEM((rows, width), f32), in_specs...  73.5 us
    add x1, other arithmetic, small_body(): ema_next = 0.99 * hess_ema + 0.01 * hess_diag  4.54 us

profile of v5, /device:TPU:0, one launch (start us, length us, event | category | flops | bytes accessed | tf_op | source)
XLA Modules:
  0.0 78.8 jit_solution(15420660103413225304)
XLA Ops:
  0.6 0.0 copy-start.1
  0.6 0.0 copy-start
  0.7 73.5 %shard_map.77 = f32[640,1792]{1,0:T(8,128)S(1)} custom-call(bf16[32,2560]{1,0:T(8,128)(2,1)} %tokens.1, bf16[256,1792]{1,0:T(8,128)(2,1)} %cotangent.1, bf16[256,1792]{1,0:T(8,128)(2,1)} %up_branch.1, bf16[640,1792]{1,0:T(8,128)(2,1)} %gate_weight.1, bf16[640,1792]{1,0:T(8,128)(2,1)} %probe.1), custom_call_target="tpu_custom_call" | custom-call | flops 7000000000 | bytes 12000000 | tf_op jit(solution)/shard_map/pallas_call | solution.py:361
  74.2 0.0 copy-done.1
  74.2 0.0 copy-done
  74.2 4.5 %multiply_add_fusion = (f32[640,1792]{1,0:T(8,128)}, f32[640,1792]{1,0:T(8,128)}) fusion(f32[640,1792]{1,0:T(8,128)S(1)} %copy-done, f32[640,1792]{1,0:T(8,128)S(1)} %shard_map.77, bf16[640,1792]{1,0:T(8,128)(2,1)S(1)} %copy-done.1), kind=kLoop, calls=%fused_computation | loop fusion | flops 5734400 | bytes 20643840 | tf_op jit(solution)/shard_map/add | solution.py:394
Async XLA Ops:
  0.6 73.6 %copy-start.1 = (bf16[640,1792]{1,0:T(8,128)(2,1)S(1)}, bf16[640,1792]{1,0:T(8,128)(2,1)}, u32[]{:S(2)}) copy-start(bf16[640,1792]{1,0:T(8,128)(2,1)} %probe.1) | copy-start | bytes 6881284
  0.6 73.6 %copy-start = (f32[640,1792]{1,0:T(8,128)S(1)}, f32[640,1792]{1,0:T(8,128)}, u32[]{:S(2)}) copy-start(f32[640,1792]{1,0:T(8,128)} %param.11) | copy-start | bytes 13762564
